TPU v7x, 512 devices: a whole 4x8x8 slice. The times are simulated.
512 devices in a mesh: smp: 8 (over x, y_hi), proto: 64 (over y_lo, z, core).
Axes of the slice: x: 4, y: 8 (y_hi: 2, y_lo: 4; y = y_hi * 4 + y_lo), z: 8, core: 2. Of those that a mesh axis runs over, the one named last changes fastest.
Arguments:
- teacher_features: bfloat16 [1024, 512], P('smp', 'proto'), may hold values from -6 to 6
- student_features: bfloat16 [1024, 512], P('smp', 'proto'), may hold values from -6 to 6
- teacher_weight: bfloat16 [131072, 512], P('proto'), may hold values from -0.45 to 0.45
- student_weight: bfloat16 [131072, 512], P('proto'), may hold values from -0.19921875 to 0.19921875
Outputs:
- sample_loss: float32 [1024], P('smp')
- grad_features: float32 [1024, 512], P('smp', 'proto')
- grad_weight: float32 [131072, 512], P('proto', 'smp')
All inputs are finite; a program needn't handle non-finite values.
Results may differ from a plain program's by a relative error of at most 0.0085.
Values may be sent and summed in bfloat16 or wider, within the bound.
No kernel may reach another device: no remote copies, remote signals or barrier semaphores. Data moves between devices by JAX's collectives and lax.ppermute only.
A program may use at most 64 MiB of HBM per device.

v0:
```python
import jax
import jax.numpy as jnp
from jax import lax
from jax.sharding import PartitionSpec as P

ITERS = 3
TEACHER_TEMP = 0.07
STUDENT_TEMP = 0.1


def sent_to_all(x, axis):
    count = lax.axis_size(axis)
    return lax.all_to_all(jnp.broadcast_to(x[None], (count, *x.shape)), axis, 0, 0, tiled=True)


def taken_together(x, axis):
    return sent_to_all(x, axis).sum(axis=0)


def packed_total(arrays, axis):
    flat, at, done = (jnp.concatenate([a.reshape(-1) for a in arrays]), 0, [])
    total = taken_together(flat, axis)
    for a in arrays:
        done.append(total[at : at + a.size].reshape(a.shape))
        at += a.size
    return tuple(done)


def turned_gather(arrays, axis, dims):
    turned = [jnp.moveaxis(a, dim, 0) for a, dim in zip(arrays, dims)]
    widths = [t[0].size for t in turned]
    both = jnp.concatenate([t.reshape(-1, w) for t, w in zip(turned, widths)], axis=1)
    whole = lax.all_gather(both, axis, axis=0, tiled=True)
    pieces = jnp.split(whole, [sum(widths[:k]) for k in range(1, len(widths))], axis=1)
    return tuple(
        (
            jnp.moveaxis(b.reshape(-1, *t.shape[1:]), 0, dim)
            for b, t, dim in zip(pieces, turned, dims)
        )
    )


def cut_along(x, dim, count):
    before, after = (x.shape[:dim], x.shape[dim + 1 :])
    return jnp.moveaxis(x.reshape(*before, count, -1, *after), dim, 0)


def sent_and_summed(x, axis, dim):
    count = lax.axis_size(axis)
    pieces = lax.all_to_all(cut_along(x, dim, count), axis, 0, 0, tiled=True)
    return jnp.sum(pieces.astype(jnp.float32), axis=0)


def sum_at_owner(x, axis, dim):
    pieces = cut_along(x, dim, lax.axis_size(axis))
    arrived = lax.all_to_all(pieces, axis, split_axis=0, concat_axis=0, tiled=True)
    return arrived.sum(axis=0)


def unit_rows(features):
    values = features.astype(jnp.float32)
    scale = lax.rsqrt(jnp.sum(values * values, axis=1) + 1e-06)
    return ((values * scale[:, None]).astype(jnp.bfloat16), scale)


def project(rows, weight):
    return lax.dot_general(
        rows, weight, (((1,), (1,)), ((), ())), preferred_element_type=jnp.float32
    )


def sample_totals(values):
    return (taken_together(values[0], "proto"),)


def student_totals(values):
    return packed_total((values[0], values[1]), "proto")


def on_device(teacher_features, student_features, teacher_weight, student_weight):
    teacher_all, student_all = turned_gather((teacher_features, student_features), "proto", (1, 1))
    sample_rows = teacher_features.shape[0]
    proto_rows = teacher_weight.shape[0]
    samples = sample_rows * lax.axis_size("smp")
    protos = proto_rows * lax.axis_size("proto")
    teacher_unit, unused = unit_rows(teacher_all)
    student_unit, student_scale = unit_rows(student_all)
    kernel = jnp.exp(project(teacher_unit, teacher_weight) / TEACHER_TEMP)
    col_scale = jnp.ones((sample_rows,), jnp.float32)
    row_scale = jnp.ones((proto_rows,), jnp.float32)
    exp_total = None
    for step in range(ITERS):
        proto_mass = jnp.dot(col_scale, kernel, precision=lax.Precision.HIGHEST)
        row_scale = 1.0 / (protos * taken_together(proto_mass, "smp"))
        sample_part = jnp.dot(kernel, row_scale, precision=lax.Precision.HIGHEST)
        sample_mass = sample_totals((sample_part,))[0]
        col_scale = 1.0 / (samples * sample_mass)
    targets = samples * kernel * row_scale[None, :] * col_scale[:, None]
    logits = project(student_unit, student_weight) / STUDENT_TEMP
    expo = jnp.exp(logits)
    logits, expo, local_total = (logits, expo, jnp.sum(expo, axis=1))
    weighted = jnp.sum(targets * logits, axis=1)
    exp_total, weighted_total = student_totals((local_total, weighted))
    probs = expo / exp_total[:, None]
    sample_loss = jnp.log(exp_total) - weighted_total
    logit_grad = ((probs - targets) / (samples * STUDENT_TEMP)).astype(jnp.bfloat16)
    weight_part = lax.dot_general(
        logit_grad, student_unit, (((0,), (0,)), ((), ())), preferred_element_type=jnp.float32
    )
    grad_weight = sent_and_summed(weight_part.astype(jnp.bfloat16), "smp", 1)
    unit_part = jnp.dot(logit_grad, student_weight, preferred_element_type=jnp.float32)
    unit_grad = sum_at_owner(unit_part, "proto", 1)
    feats = student_features.astype(jnp.float32)
    inner_prod = taken_together(jnp.sum(feats * unit_grad, axis=1), "proto")
    grad_features = (
        student_scale[:, None] * unit_grad - (student_scale**3 * inner_prod)[:, None] * feats
    )
    return (sample_loss, grad_features, grad_weight)


def solution(mesh):
    placed = (P("smp", "proto"), P("smp", "proto"), P("proto", None), P("proto", None))
    return jax.shard_map(
        on_device,
        mesh=mesh,
        in_specs=placed,
        out_specs=(P("smp"), P("smp", "proto"), P("proto", "smp")),
        check_vma=False,
    )
```

profile of v0, /device:TPU:8, one launch (start us, length us, event | category | flops | bytes accessed | tf_op | source)
XLA Modules:
  0.0 290.4 jit_solution(18363776780646376817)
XLA Ops:
  0.6 0.0 copy-start
  0.6 0.9 pad_maximum_fusion
  1.5 71.8 %all_gather.3 = bf16[512,256]{1,0:T(8,128)(2,1)S(1)} all-gather(bf16[8,256]{1,0:T(8,128)(2,1)S(1)} %pad_maximum_fusion), channel_id=1, replica_groups=mesh['smp'=8,'proto'=64] {'proto'}, dimensions={0}, use_global_device_ids=true | all-gather | bytes 266240 | tf_op jit(solution)/shard_map/all_gather | solution.py:33
  73.3 0.1 fusion.3
  73.4 2.4 fusion
  75.8 0.6 fusion.21
  76.5 17.3 %all_to_all.58 = f32[8,1,2048]{2,1,0:T(1,128)S(1)} all-to-all(f32[8,1,2048]{2,1,0:T(1,128)S(1)} %broadcast_in_dim.16), channel_id=1, replica_groups=mesh['smp'=8,'proto'=64] {'smp'}, dimensions={0} | all-to-all | bytes 131072 | tf_op jit(solution)/shard_map/all_to_all | solution.py:13
  93.7 0.1 reduce_sum.138
  93.8 0.9 convolution_bitcast_fusion.3
  94.8 27.2 %all_to_all.59 = f32[64,1,128]{2,1,0:T(1,128)S(1)} all-to-all(f32[64,1,128]{2,1,0:T(1,128)S(1)} %broadcast_in_dim.17), channel_id=1, replica_groups=mesh['smp'=8,'proto'=64] {'proto'}, dimensions={0} | all-to-all | bytes 65536 | tf_op jit(solution)/shard_map/all_to_all | solution.py:13
  122.0 0.6 fusion.15
  122.6 12.9 %all_to_all.60 = f32[8,1,2048]{2,1,0:T(1,128)S(1)} all-to-all(f32[8,1,2048]{2,1,0:T(1,128)S(1)} %broadcast_in_dim.18), channel_id=1, replica_groups=mesh['smp'=8,'proto'=64] {'smp'}, dimensions={0} | all-to-all | bytes 131072 | tf_op jit(solution)/shard_map/all_to_all | solution.py:13
  135.5 0.1 reduce_sum.140
  135.6 0.9 convolution_bitcast_fusion.2
  136.6 13.4 %all_to_all.61 = f32[64,1,128]{2,1,0:T(1,128)S(1)} all-to-all(f32[64,1,128]{2,1,0:T(1,128)S(1)} %broadcast_in_dim.19), channel_id=1, replica_groups=mesh['smp'=8,'proto'=64] {'proto'}, dimensions={0} | all-to-all | bytes 65536 | tf_op jit(solution)/shard_map/all_to_all | solution.py:13
  150.0 0.6 fusion.13
  150.6 12.9 %all_to_all.62 = f32[8,1,2048]{2,1,0:T(1,128)S(1)} all-to-all(f32[8,1,2048]{2,1,0:T(1,128)S(1)} %broadcast_in_dim.20), channel_id=1, replica_groups=mesh['smp'=8,'proto'=64] {'smp'}, dimensions={0} | all-to-all | bytes 131072 | tf_op jit(solution)/shard_map/all_to_all | solution.py:13
  163.5 0.1 reduce_sum.142
  163.6 0.9 convolution_bitcast_fusion.1
  164.6 13.4 %all_to_all.63 = f32[64,1,128]{2,1,0:T(1,128)S(1)} all-to-all(f32[64,1,128]{2,1,0:T(1,128)S(1)} %broadcast_in_dim.21), channel_id=1, replica_groups=mesh['smp'=8,'proto'=64] {'proto'}, dimensions={0} | all-to-all | bytes 65536 | tf_op jit(solution)/shard_map/all_to_all | solution.py:13
  178.0 0.0 copy-done
  178.0 1.8 exponential_reduce_fusion
  179.9 13.7 %all_to_all.64 = f32[64,1,256]{2,1,0:T(1,128)S(1)} all-to-all(f32[64,1,256]{2,1,0:T(1,128)S(1)} %broadcast_in_dim.22), channel_id=1, replica_groups=mesh['smp'=8,'proto'=64] {'proto'}, dimensions={0} | all-to-all | bytes 131072 | tf_op jit(solution)/shard_map/all_to_all | solution.py:13
  193.6 0.1 reduce_sum.145
  193.7 0.5 fusion.32
  194.2 1.5 multiply_convert_fusion
  195.8 0.0 copy-start.1
  195.8 0.8 copy-done.1
  196.6 0.0 copy-start.2
  196.6 0.9 convolution_bitcast_fusion
  197.5 16.8 %all_to_all.65 = f32[64,128,8]{1,2,0:T(8,128)S(1)} all-to-all(f32[64,128,8]{1,2,0:T(8,128)S(1)} %convolution_bitcast_fusion), channel_id=1, replica_groups=mesh['smp'=8,'proto'=64] {'proto'}, dimensions={0} | all-to-all | bytes 524288 | tf_op jit(solution)/shard_map/all_to_all | solution.py:56
  214.3 0.1 reduce_sum.146
  214.4 0.0 copy-done.2
  214.4 0.6 broadcast_in_dim.23
  215.0 5.7 %all-to-all-start.8 = ((f32[64,1,128]{2,1,0:T(1,128)}), f32[64,1,128]{2,1,0:T(1,128)S(1)}, u32[]{:S(2)}, u32[]{:S(2)}) async-start(f32[64,1,128]{2,1,0:T(1,128)} %broadcast_in_dim.23), calls=%async_computation.8 | async-start | bytes 65536 | tf_op jit(solution)/shard_map/all_to_all | solution.py:13
  220.7 3.1 %convolution_convert_fusion = bf16[2048,512]{0,1:T(8,128)(2,1)} fusion(bf16[128,2048]{1,0:T(8,128)(2,1)} %copy-done.1, f32[128]{0:T(128)S(1)} %get-tuple-element.13, bf16[512,256]{1,0:T(8,128)(2,1)S(1)} %all_gather.3), kind=kOutput, calls=%fused_computation.1 | convolution fusion | flops 269680640 | bytes 2753024 | tf_op jit(solution)/shard_map/dot_general | solution.py:107
  223.8 5.8 %all-to-all-done.8 = f32[64,1,128]{2,1,0:T(1,128)S(1)} async-done(((f32[64,1,128]{2,1,0:T(1,128)}), f32[64,1,128]{2,1,0:T(1,128)S(1)}, u32[]{:S(2)}, u32[]{:S(2)}) %all-to-all-start.8) | async-done | bytes 32800 | tf_op jit(solution)/shard_map/all_to_all | solution.py:13
  229.6 4.4 %all-to-all-start.9 = ((bf16[8,2048,64]{1,2,0:T(8,128)(2,1)}), bf16[8,2048,64]{1,2,0:T(8,128)(2,1)}, u32[]{:S(2)}, u32[]{:S(2)}) async-start(bf16[8,2048,64]{1,2,0:T(8,128)(2,1)} %bitcast.45), calls=%async_computation.9 | async-start | bytes 4194304 | tf_op jit(solution)/shard_map/all_to_all | solution.py:50
  234.0 0.6 fusion.11
  234.6 53.0 %all-to-all-done.9 = bf16[8,2048,64]{1,2,0:T(8,128)(2,1)} async-done(((bf16[8,2048,64]{1,2,0:T(8,128)(2,1)}), bf16[8,2048,64]{1,2,0:T(8,128)(2,1)}, u32[]{:S(2)}, u32[]{:S(2)}) %all-to-all-start.9) | async-done | bytes 2097184 | tf_op jit(solution)/shard_map/all_to_all | solution.py:50
  287.6 2.8 convert_reduce_fusion
  (19 shorter events, 0.4 us)
Async XLA Ops:
  0.6 177.3 %copy-start = (bf16[2048,512]{1,0:T(8,128)(2,1)S(1)}, bf16[2048,512]{1,0:T(8,128)(2,1)}, u32[]{:S(2)}) copy-start(bf16[2048,512]{1,0:T(8,128)(2,1)} %param.7) | copy-start | bytes 6291460
  195.8 0.8 copy-start.1
  196.6 17.8 %copy-start.2 = (bf16[128,8]{0,1:T(8,128)(2,1)S(1)}, bf16[128,8]{0,1:T(8,128)(2,1)}, u32[]{:S(2)}) copy-start(bf16[128,8]{0,1:T(8,128)(2,1)} %param.5) | copy-start | bytes 6148
  215.0 14.5 %all-to-all-start.8 = ((f32[64,1,128]{2,1,0:T(1,128)}), f32[64,1,128]{2,1,0:T(1,128)S(1)}, u32[]{:S(2)}, u32[]{:S(2)}) async-start(f32[64,1,128]{2,1,0:T(1,128)} %broadcast_in_dim.23), calls=%async_computation.8 | async-start | bytes 65536 | tf_op jit(solution)/shard_map/all_to_all | solution.py:13
  229.6 58.0 %all-to-all-start.9 = ((bf16[8,2048,64]{1,2,0:T(8,128)(2,1)}), bf16[8,2048,64]{1,2,0:T(8,128)(2,1)}, u32[]{:S(2)}, u32[]{:S(2)}) async-start(bf16[8,2048,64]{1,2,0:T(8,128)(2,1)} %bitcast.45), calls=%async_computation.9 | async-start | bytes 4194304 | tf_op jit(solution)/shard_map/all_to_all | solution.py:50
where the time goes:
time: 291 us; the launch traced here: 290 us
  blocking collectives  199 us (68%)
  waiting for transfers between devices  58.8 us (20%)
  matrix products  12.9 us (4%)
  starting transfers between devices  10 us (3%)
  other arithmetic  6.86 us (2%)
    all_to_all x7, blocking collectives, sent_to_all(): lax.all_to_all(jnp.broadcast_to(x[None], (count, *x.shape)), axis, 0, 0,...  111 us
    all_gather x1, blocking collectives, turned_gather(): whole = lax.all_gather(both, axis, axis=0, tiled=True)  71.8 us
    all_to_all x1, waiting for transfers between devices, sent_and_summed(): pieces = lax.all_to_all(cut_along(x, dim, count), axis, 0, 0, tiled=True)  53 us
    all_to_all x1, blocking collectives, sum_at_owner(): lax.all_to_all(pieces, axis, split_axis=0, concat_axis=0, tiled=True)  16.8 us
  transfers between devices with their start and end apart: 2, of which 2 were waited for; matrix products, arithmetic and copies ran while one was open for 1% of the time, Pallas kernels for 0%

commit v1 on v0

--- a/solution.py
+++ b/solution.py
@@ -30,7 +30,10 @@
     turned = [jnp.moveaxis(a, dim, 0) for a, dim in zip(arrays, dims)]
     widths = [t[0].size for t in turned]
     both = jnp.concatenate([t.reshape(-1, w) for t, w in zip(turned, widths)], axis=1)
-    whole = lax.all_gather(both, axis, axis=0, tiled=True)
+    n_dev = lax.axis_size(axis)
+    tiles = jnp.stack([both for _ in range(n_dev)])
+    tiles = lax.all_to_all(tiles, axis, split_axis=0, concat_axis=0)
+    whole = jnp.concatenate(tiles, axis=0)
     pieces = jnp.split(whole, [sum(widths[:k]) for k in range(1, len(widths))], axis=1)
     return tuple(
         (

time: 291 us -> 232 us (0.80)
  blocking collectives: 199 us -> 140 us
    all_gather x1 -> x0, blocking collectives: 71.8 us -> none  [turned_gather(): whole = lax.all_gather(both, axis, axis=0, tiled=True)]
    all_to_all x0 -> x1, blocking collectives: none -> 26.1 us  [turned_gather(): tiles = lax.all_to_all(tiles, axis, split_axis=0, concat_axis=0)]
    all_to_all x7, blocking collectives: 111 us -> 97.6 us  [sent_to_all(): lax.all_to_all(jnp.broadcast_to(x[None], (count, *x.shape)), axis, 0, 0,...]
  transfers between devices with their start and end apart: 2 -> 2, of which waited for: 2 -> 2; matrix products, arithmetic and copies ran while one was open for 1% -> 2% of each run, Pallas kernels for 0% -> 0%
where the time goes in v1:
time: 232 us; the launch traced here: 231 us
  blocking collectives  140 us (60%)
  waiting for transfers between devices  58.8 us (25%)
  matrix products  12.9 us (6%)
  starting transfers between devices  10 us (4%)
  other arithmetic  6.86 us (3%)
    all_to_all x7, blocking collectives, sent_to_all(): lax.all_to_all(jnp.broadcast_to(x[None], (count, *x.shape)), axis, 0, 0,...  97.6 us
    all_to_all x1, waiting for transfers between devices, sent_and_summed(): pieces = lax.all_to_all(cut_along(x, dim, count), axis, 0, 0, tiled=True)  53 us
    all_to_all x1, blocking collectives, turned_gather(): tiles = lax.all_to_all(tiles, axis, split_axis=0, concat_axis=0)  26.1 us
    all_to_all x1, blocking collectives, sum_at_owner(): lax.all_to_all(pieces, axis, split_axis=0, concat_axis=0, tiled=True)  16.6 us
    all_to_all x1, waiting for transfers between devices, sent_to_all(): lax.all_to_all(jnp.broadcast_to(x[None], (count, *x.shape)), axis, 0, 0,...  5.78 us
    all_to_all x1, starting transfers between devices, sent_to_all(): lax.all_to_all(jnp.broadcast_to(x[None], (count, *x.shape)), axis, 0, 0,...  5.66 us
  transfers between devices with their start and end apart: 2, of which 2 were waited for; matrix products, arithmetic and copies ran while one was open for 2% of the time, Pallas kernels for 0%

profile of v1, /device:TPU:8, one launch (start us, length us, event | category | flops | bytes accessed | tf_op | source)
XLA Modules:
  0.0 231.3 jit_solution(14418264967514713911)
XLA Ops:
  0.6 0.0 copy-start
  0.6 0.9 pad_maximum_fusion
  1.5 26.1 %all_to_all.63 = bf16[64,8,256]{2,1,0:T(8,128)(2,1)S(1)} all-to-all(bf16[64,8,256]{2,1,0:T(8,128)(2,1)S(1)} %stack.2), channel_id=1, replica_groups=mesh['smp'=8,'proto'=64] {'proto'}, dimensions={0} | all-to-all | bytes 524288 | tf_op jit(solution)/shard_map/all_to_all | solution.py:35
  27.6 0.1 fusion.3
  27.7 2.4 %fusion = f32[128,2048]{1,0:T(8,128)S(1)} fusion(bf16[2048,512]{1,0:T(8,128)(2,1)} %param.6, f32[128]{0:T(128)S(1)} %get-tuple-element.12, bf16[512,256]{1,0:T(8,128)(2,1)S(1)} %bitcast.48), kind=kOutput, calls=%fused_computation.3 | convolution fusion | flops 268894208 | bytes 3277312 | tf_op jit(solution)/shard_map/dot_general | solution.py:70
  30.2 0.6 fusion.21
  30.8 16.9 %all_to_all.64 = f32[8,1,2048]{2,1,0:T(1,128)S(1)} all-to-all(f32[8,1,2048]{2,1,0:T(1,128)S(1)} %broadcast_in_dim.16), channel_id=1, replica_groups=mesh['smp'=8,'proto'=64] {'smp'}, dimensions={0} | all-to-all | bytes 131072 | tf_op jit(solution)/shard_map/all_to_all | solution.py:13
  47.7 0.1 reduce_sum.138
  47.8 0.9 convolution_bitcast_fusion.3
  48.7 14.3 %all_to_all.65 = f32[64,1,128]{2,1,0:T(1,128)S(1)} all-to-all(f32[64,1,128]{2,1,0:T(1,128)S(1)} %broadcast_in_dim.17), channel_id=1, replica_groups=mesh['smp'=8,'proto'=64] {'proto'}, dimensions={0} | all-to-all | bytes 65536 | tf_op jit(solution)/shard_map/all_to_all | solution.py:13
  63.1 0.6 fusion.15
  63.8 12.9 %all_to_all.66 = f32[8,1,2048]{2,1,0:T(1,128)S(1)} all-to-all(f32[8,1,2048]{2,1,0:T(1,128)S(1)} %broadcast_in_dim.18), channel_id=1, replica_groups=mesh['smp'=8,'proto'=64] {'smp'}, dimensions={0} | all-to-all | bytes 131072 | tf_op jit(solution)/shard_map/all_to_all | solution.py:13
  76.7 0.1 reduce_sum.140
  76.7 0.9 convolution_bitcast_fusion.2
  77.7 13.4 %all_to_all.67 = f32[64,1,128]{2,1,0:T(1,128)S(1)} all-to-all(f32[64,1,128]{2,1,0:T(1,128)S(1)} %broadcast_in_dim.19), channel_id=1, replica_groups=mesh['smp'=8,'proto'=64] {'proto'}, dimensions={0} | all-to-all | bytes 65536 | tf_op jit(solution)/shard_map/all_to_all | solution.py:13
  91.1 0.6 fusion.13
  91.7 12.9 %all_to_all.68 = f32[8,1,2048]{2,1,0:T(1,128)S(1)} all-to-all(f32[8,1,2048]{2,1,0:T(1,128)S(1)} %broadcast_in_dim.20), channel_id=1, replica_groups=mesh['smp'=8,'proto'=64] {'smp'}, dimensions={0} | all-to-all | bytes 131072 | tf_op jit(solution)/shard_map/all_to_all | solution.py:13
  104.7 0.1 reduce_sum.142
  104.7 0.9 convolution_bitcast_fusion.1
  105.7 13.4 %all_to_all.69 = f32[64,1,128]{2,1,0:T(1,128)S(1)} all-to-all(f32[64,1,128]{2,1,0:T(1,128)S(1)} %broadcast_in_dim.21), channel_id=1, replica_groups=mesh['smp'=8,'proto'=64] {'proto'}, dimensions={0} | all-to-all | bytes 65536 | tf_op jit(solution)/shard_map/all_to_all | solution.py:13
  119.1 0.0 copy-done
  119.1 1.8 exponential_reduce_fusion
  121.0 13.7 %all_to_all.70 = f32[64,1,256]{2,1,0:T(1,128)S(1)} all-to-all(f32[64,1,256]{2,1,0:T(1,128)S(1)} %broadcast_in_dim.22), channel_id=1, replica_groups=mesh['smp'=8,'proto'=64] {'proto'}, dimensions={0} | all-to-all | bytes 131072 | tf_op jit(solution)/shard_map/all_to_all | solution.py:13
  134.7 0.1 reduce_sum.145
  134.8 0.5 fusion.32
  135.3 1.5 multiply_convert_fusion
  136.9 0.0 copy-start.1
  136.9 0.8 copy-done.1
  137.7 0.0 copy-start.2
  137.7 0.9 convolution_bitcast_fusion
  138.6 16.6 %all_to_all.71 = f32[64,128,8]{1,2,0:T(8,128)S(1)} all-to-all(f32[64,128,8]{1,2,0:T(8,128)S(1)} %convolution_bitcast_fusion), channel_id=1, replica_groups=mesh['smp'=8,'proto'=64] {'proto'}, dimensions={0} | all-to-all | bytes 524288 | tf_op jit(solution)/shard_map/all_to_all | solution.py:59
  155.3 0.1 reduce_sum.146
  155.3 0.0 copy-done.2
  155.4 0.6 broadcast_in_dim.23
  156.0 5.7 %all-to-all-start.9 = ((f32[64,1,128]{2,1,0:T(1,128)}), f32[64,1,128]{2,1,0:T(1,128)S(1)}, u32[]{:S(2)}, u32[]{:S(2)}) async-start(f32[64,1,128]{2,1,0:T(1,128)} %broadcast_in_dim.23), calls=%async_computation.9 | async-start | bytes 65536 | tf_op jit(solution)/shard_map/all_to_all | solution.py:13
  161.6 3.1 %convolution_convert_fusion = bf16[2048,512]{0,1:T(8,128)(2,1)} fusion(bf16[128,2048]{1,0:T(8,128)(2,1)} %copy-done.1, f32[128]{0:T(128)S(1)} %get-tuple-element.13, bf16[512,256]{1,0:T(8,128)(2,1)S(1)} %bitcast.50), kind=kOutput, calls=%fused_computation.1 | convolution fusion | flops 269680640 | bytes 2753024 | tf_op jit(solution)/shard_map/dot_general | solution.py:110
  164.7 5.8 %all-to-all-done.9 = f32[64,1,128]{2,1,0:T(1,128)S(1)} async-done(((f32[64,1,128]{2,1,0:T(1,128)}), f32[64,1,128]{2,1,0:T(1,128)S(1)}, u32[]{:S(2)}, u32[]{:S(2)}) %all-to-all-start.9) | async-done | bytes 32800 | tf_op jit(solution)/shard_map/all_to_all | solution.py:13
  170.5 4.4 %all-to-all-start.10 = ((bf16[8,2048,64]{1,2,0:T(8,128)(2,1)}), bf16[8,2048,64]{1,2,0:T(8,128)(2,1)}, u32[]{:S(2)}, u32[]{:S(2)}) async-start(bf16[8,2048,64]{1,2,0:T(8,128)(2,1)} %bitcast.46), calls=%async_computation.10 | async-start | bytes 4194304 | tf_op jit(solution)/shard_map/all_to_all | solution.py:53
  174.9 0.6 fusion.11
  175.5 53.0 %all-to-all-done.10 = bf16[8,2048,64]{1,2,0:T(8,128)(2,1)} async-done(((bf16[8,2048,64]{1,2,0:T(8,128)(2,1)}), bf16[8,2048,64]{1,2,0:T(8,128)(2,1)}, u32[]{:S(2)}, u32[]{:S(2)}) %all-to-all-start.10) | async-done | bytes 2097184 | tf_op jit(solution)/shard_map/all_to_all | solution.py:53
  228.6 2.8 %convert_reduce_fusion = f32[2048,64]{0,1:T(8,128)} fusion(bf16[8,2048,64]{1,2,0:T(8,128)(2,1)} %all-to-all-done.10), kind=kLoop, calls=%fused_computation | loop fusion | flops 1966080 | bytes 2621440 | tf_op jit(solution)/shard_map/reduce_sum | solution.py:54
  (20 shorter events, 0.4 us)
Async XLA Ops:
  0.6 118.5 %copy-start = (bf16[2048,512]{1,0:T(8,128)(2,1)S(1)}, bf16[2048,512]{1,0:T(8,128)(2,1)}, u32[]{:S(2)}) copy-start(bf16[2048,512]{1,0:T(8,128)(2,1)} %param.7) | copy-start | bytes 6291460
  136.9 0.8 copy-start.1
  137.7 17.7 %copy-start.2 = (bf16[128,8]{0,1:T(8,128)(2,1)S(1)}, bf16[128,8]{0,1:T(8,128)(2,1)}, u32[]{:S(2)}) copy-start(bf16[128,8]{0,1:T(8,128)(2,1)} %param.5) | copy-start | bytes 6148
  156.0 14.5 %all-to-all-start.9 = ((f32[64,1,128]{2,1,0:T(1,128)}), f32[64,1,128]{2,1,0:T(1,128)S(1)}, u32[]{:S(2)}, u32[]{:S(2)}) async-start(f32[64,1,128]{2,1,0:T(1,128)} %broadcast_in_dim.23), calls=%async_computation.9 | async-start | bytes 65536 | tf_op jit(solution)/shard_map/all_to_all | solution.py:13
  170.5 58.0 %all-to-all-start.10 = ((bf16[8,2048,64]{1,2,0:T(8,128)(2,1)}), bf16[8,2048,64]{1,2,0:T(8,128)(2,1)}, u32[]{:S(2)}, u32[]{:S(2)}) async-start(bf16[8,2048,64]{1,2,0:T(8,128)(2,1)} %bitcast.46), calls=%async_computation.10 | async-start | bytes 4194304 | tf_op jit(solution)/shard_map/all_to_all | solution.py:53
